TPU v7x, 512 devices: a whole 4x8x8 slice. The times are simulated.
512 devices in a mesh: grp: 16 (over x, z_lo), mem: 32 (over z_hi, y, core).
Axes of the slice: x: 4, y: 8, z: 8 (z_hi: 2, z_lo: 4; z = z_hi * 4 + z_lo), core: 2. Of those that a mesh axis runs over, the one named last changes fastest.
Arguments:
- points: float32 [16, 262144], P(None, ('grp', 'mem')), may hold values from -6 to 6
- lengthscales: float32 [16], replicated, may hold values from 3 to 12
- probes: float32 [8, 262144], P(None, ('grp', 'mem')), may hold values from -0.25 to 0.25
- plan: int32 [16, 16], replicated, may hold values from 0 to 15, as said below
- round_index: int32 [1], replicated, may hold values from 0 to 15
Outputs:
- product: float32 [8, 262144], P(None, ('grp', 'mem'))
Inputs may be any that keep to these rules, and one draw needn't show every extreme that they name: plan[r, g] = g XOR t_r for one t_r of 1 to 15 in each round r, the same for all g, so that each round's pairing is a perfect matching without fixed points.
All inputs are finite; a program needn't handle non-finite values.
Results may differ from a plain program's by a relative error of at most 0.0003.
Values sent between devices are 32-bit elements; how exact they have to be, the bound alone decides.
A program may use at most 64 MiB of HBM per device.

v0:
```python
import math

import jax
import jax.numpy as jnp
from jax import lax
from jax.sharding import PartitionSpec as P

ROOT_FIVE = math.sqrt(5.0)


def swapped(x, axis, bit):
    return lax.ppermute(x, axis, [(i, i ^ 1 << bit) for i in range(lax.axis_size(axis))])


def matern(left, right):
    cross = lax.dot_general(
        left,
        right,
        (((0,), (0,)), ((), ())),
        precision=lax.Precision.HIGHEST,
        preferred_element_type=jnp.float32,
    )
    dist_sq = (
        jnp.sum(left * left, axis=0)[:, None]
        + jnp.sum(right * right, axis=0)[None, :]
        - 2.0 * cross
    )
    scaled_dist = ROOT_FIVE * jnp.sqrt(jnp.maximum(dist_sq, 0.0))
    return (1.0 + scaled_dist + scaled_dist * scaled_dist / 3.0) * jnp.exp(-scaled_dist)


def apply_probes(vectors, kern):
    return lax.dot_general(
        vectors,
        kern,
        (((1,), (1,)), ((), ())),
        precision=lax.Precision.HIGHEST,
        preferred_element_type=jnp.float32,
    )


def shards(points, lengthscales, probes, plan, round_index):
    scaled = points / lengthscales[:, None]
    width = points.shape[1]
    pairing = plan[round_index[0]]
    offset = pairing[0]
    bit_count = lax.axis_size("grp").bit_length() - 1
    far_pts = scaled
    far_prb = probes
    for bit in range(bit_count):
        moved_pts, moved_prb = swapped((far_pts, far_prb), "grp", bit)
        flag = offset >> bit & 1 == 1
        far_pts = jnp.where(flag, moved_pts, far_pts)
        far_prb = jnp.where(flag, moved_prb, far_prb)
    start_sum = jnp.zeros((probes.shape[0], width), jnp.float32)
    cols = lax.all_gather(far_pts, "mem", axis=1, tiled=True)
    vecs = lax.all_gather(far_prb, "mem", axis=1, tiled=True)
    span = cols.shape[1]
    step = math.gcd(span, 2048)

    def inner(index, acc):
        block_pts = lax.dynamic_slice_in_dim(cols, index * step, step, 1)
        block_prb = lax.dynamic_slice_in_dim(vecs, index * step, step, 1)
        return acc + apply_probes(block_prb, matern(scaled, block_pts))

    return lax.fori_loop(0, span // step, inner, start_sum)


def solution(mesh):
    in_specs = (P(None, ("grp", "mem")), P(), P(None, ("grp", "mem")), P(), P())
    out_specs = P(None, ("grp", "mem"))
    return jax.shard_map(shards, mesh=mesh, in_specs=in_specs, out_specs=out_specs, check_vma=False)
```

profile of v0, /device:TPU:1, one launch (start us, length us, event | category | flops | bytes accessed | tf_op | source)
XLA Modules:
  0.0 217.3 jit_solution(2268124166862782251)
XLA Ops:
  6.5 0.0 copy-start
  6.5 0.0 all-gather.2.cloned.1.call-start
  6.5 0.9 multiply_reduce_fusion.1
  7.4 4.8 %collective-permute-start.4 = (f32[16,512]{1,0:T(8,128)S(1)}, f32[16,512]{1,0:T(8,128)S(1)}, u32[]{:S(2)}, u32[]{:S(2)}) collective-permute-start(f32[16,512]{1,0:T(8,128)S(1)} %get-tuple-element.216), channel_id=1, source_target_pairs={{0,32},{32,0},{64,96},{96,64},{128,160},{160,128},{192,224},{224,1... | collective-permute-start | bytes 98312 | tf_op jit(solution)/shard_map/ppermute | solution.py:12
  12.9 0.0 copy-done
  13.0 0.6 collective-permute-done.4
  13.5 5.8 %collective-permute-start.5 = (f32[16,512]{1,0:T(8,128)S(1)}, f32[16,512]{1,0:T(8,128)S(1)}, u32[]{:S(2)}, u32[]{:S(2)}) collective-permute-start(f32[16,512]{1,0:T(8,128)S(1)} %broadcast_select_fusion), channel_id=1, source_target_pairs={{0,64},{32,96},{64,0},{96,32},{128,192},{160,224},{192,128},{224,1... | collective-permute-start | bytes 98312 | tf_op jit(solution)/shard_map/ppermute | solution.py:12
  19.4 1.3 collective-permute-done.5
  20.6 3.1 %collective-permute-start.6 = (f32[16,512]{1,0:T(8,128)S(1)}, f32[16,512]{1,0:T(8,128)S(1)}, u32[]{:S(2)}, u32[]{:S(2)}) collective-permute-start(f32[16,512]{1,0:T(8,128)S(1)} %broadcast_select_fusion.1), channel_id=1, source_target_pairs={{0,128},{32,160},{64,192},{96,224},{128,0},{160,32},{192,64},{224,... | collective-permute-start | bytes 98312 | tf_op jit(solution)/shard_map/ppermute | solution.py:12
  23.8 1.5 collective-permute-done.6
  25.3 4.6 %collective-permute-start.7 = (f32[16,512]{1,0:T(8,128)S(1)}, f32[16,512]{1,0:T(8,128)S(1)}, u32[]{:S(2)}, u32[]{:S(2)}) collective-permute-start(f32[16,512]{1,0:T(8,128)S(1)} %broadcast_select_fusion.2), channel_id=1, source_target_pairs={{0,256},{32,288},{64,320},{96,352},{128,384},{160,416},{192,448},{... | collective-permute-start | bytes 98312 | tf_op jit(solution)/shard_map/ppermute | solution.py:12
  30.0 1.5 collective-permute-done.7
  31.4 0.6 broadcast_select_fusion.3
  32.1 0.0 all-gather.2.cloned.1.call-update
  32.1 3.4 %collective-permute-start = (f32[8,512]{1,0:T(8,128)}, f32[8,512]{1,0:T(8,128)S(1)}, u32[]{:S(2)}, u32[]{:S(2)}) collective-permute-start(f32[8,512]{1,0:T(8,128)} %param.9), channel_id=1, source_target_pairs={{0,32},{32,0},{64,96},{96,64},{128,160},{160,128},{192,224},{224,1... | collective-permute-start | bytes 49160 | tf_op jit(solution)/shard_map/ppermute | solution.py:12
  35.5 1.3 collective-permute-done
  36.8 0.7 broadcast_select_fusion.4
  37.5 4.4 %collective-permute-start.1 = (f32[8,512]{1,0:T(8,128)S(1)}, f32[8,512]{1,0:T(8,128)S(1)}, u32[]{:S(2)}, u32[]{:S(2)}) collective-permute-start(f32[8,512]{1,0:T(8,128)S(1)} %broadcast_select_fusion.4), channel_id=1, source_target_pairs={{0,64},{32,96},{64,0},{96,32},{128,192},{160,224},{192,128},{224,1... | collective-permute-start | bytes 49160 | tf_op jit(solution)/shard_map/ppermute | solution.py:12
  41.9 1.1 collective-permute-done.1
  43.0 3.0 %collective-permute-start.2 = (f32[8,512]{1,0:T(8,128)S(1)}, f32[8,512]{1,0:T(8,128)S(1)}, u32[]{:S(2)}, u32[]{:S(2)}) collective-permute-start(f32[8,512]{1,0:T(8,128)S(1)} %broadcast_select_fusion.5), channel_id=1, source_target_pairs={{0,128},{32,160},{64,192},{96,224},{128,0},{160,32},{192,64},{224,... | collective-permute-start | bytes 49160 | tf_op jit(solution)/shard_map/ppermute | solution.py:12
  46.1 1.4 collective-permute-done.2
  47.5 4.6 %collective-permute-start.3 = (f32[8,512]{1,0:T(8,128)S(1)}, f32[8,512]{1,0:T(8,128)S(1)}, u32[]{:S(2)}, u32[]{:S(2)}) collective-permute-start(f32[8,512]{1,0:T(8,128)S(1)} %broadcast_select_fusion.6), channel_id=1, source_target_pairs={{0,256},{32,288},{64,320},{96,352},{128,384},{160,416},{192,448},{... | collective-permute-start | bytes 49160 | tf_op jit(solution)/shard_map/ppermute | solution.py:12
  52.1 1.4 collective-permute-done.3
  53.5 67.7 %all_gather.6 = f32[8,16384]{1,0:T(8,128)S(1)} all-gather(f32[8,512]{1,0:T(8,128)S(1)} %broadcast_select_fusion.7), channel_id=1, replica_groups=mesh['grp'=16,'mem'=32] {'mem'}, dimensions={1}, use_global_device_ids=true | all-gather | bytes 540672 | tf_op jit(solution)/shard_map/all_gather | solution.py:57
  121.2 7.4 %all-gather.2.cloned.1.call-done = f32[16,16384]{1,0:T(8,128)} async-done(((f32[16,512]{1,0:T(8,128)}), f32[16,16384]{1,0:T(8,128)}) %all-gather.2.cloned.1.call-update) | async-done | bytes 1048592 | tf_op jit(solution)/shard_map/all_gather | solution.py:56
  128.7 81.2 %while.16 = (s32[]{:T(128)}, f32[8,512]{1,0:T(8,128)S(1)}, f32[8,16384]{1,0:T(8,128)S(1)}, f32[512]{0:T(512)S(1)}, f32[16,16384]{1,0:T(8,128)}, /*index=5*/f32[1...) while((s32[]{:T(128)}, f32[8,512]{1,0:T(8,128)S(1)}, f32[8,16384]{1,0:T(8,128)S(1)}, ...), condition=%wide.region_3.4_spmd.clone, body=%wide.region_1.0_spmd.clone.sunk | while | flops 313595904 | bytes 8800433 | solution.py:66
  128.7 0.9 multiply_reduce_fusion.3
  129.6 4.4 %fusion.45 = f32[2048,512]{1,0:T(8,128)S(1)} fusion(f32[16,512]{1,0:T(8,128)S(1)} %get-tuple-element.236, f32[16,16384]{1,0:T(8,128)} %get-tuple-element.235, s32[]{:T(128)S(6)} %select_n.100), kind=kOutput, calls=%fused_computation.23.clone.1 | convolution fusion | flops 201326592 | bytes 4358148 | tf_op jit(solution)/shard_map/while/body/eval_jaxpr/dot_general | solution.py:16
  134.0 4.8 %fusion.46 = f32[8,512]{1,0:T(8,128)S(1)} fusion(f32[2048,512]{1,0:T(8,128)S(1)} %fusion.45, f32[2048]{0:T(1024)S(1)} %multiply_reduce_fusion.3, f32[512]{0:T(512)S(1)} %get-tuple-element.234, f32[8,16384]{1,0:T(8,128)S(1)} %get-tuple-element.233, s32[]{:T(128)S(6)} %select_n.100, f32[8,512]{1,0:T(8,128)S(1)} %get-tuple-element.222, pred[]{:T(512)S(6)} %compare.3), kind=kOutput, calls=%fused_computation.21.clone.1 | convolution fusion | flops 112205824 | bytes 4302853 | tf_op jit(solution)/shard_map/while/body/eval_jaxpr/dot_general | solution.py:33
  138.8 0.9 multiply_reduce_fusion.3
  139.7 4.4 %fusion.45 = f32[2048,512]{1,0:T(8,128)S(1)} fusion(f32[16,512]{1,0:T(8,128)S(1)} %get-tuple-element.236, f32[16,16384]{1,0:T(8,128)} %get-tuple-element.235, s32[]{:T(128)S(6)} %select_n.100), kind=kOutput, calls=%fused_computation.23.clone.1 | convolution fusion | flops 201326592 | bytes 4358148 | tf_op jit(solution)/shard_map/while/body/eval_jaxpr/dot_general | solution.py:16
  144.1 4.8 %fusion.46 = f32[8,512]{1,0:T(8,128)S(1)} fusion(f32[2048,512]{1,0:T(8,128)S(1)} %fusion.45, f32[2048]{0:T(1024)S(1)} %multiply_reduce_fusion.3, f32[512]{0:T(512)S(1)} %get-tuple-element.234, f32[8,16384]{1,0:T(8,128)S(1)} %get-tuple-element.233, s32[]{:T(128)S(6)} %select_n.100, f32[8,512]{1,0:T(8,128)S(1)} %get-tuple-element.222, pred[]{:T(512)S(6)} %compare.3), kind=kOutput, calls=%fused_computation.21.clone.1 | convolution fusion | flops 112205824 | bytes 4302853 | tf_op jit(solution)/shard_map/while/body/eval_jaxpr/dot_general | solution.py:33
  148.9 0.9 multiply_reduce_fusion.3
  149.9 4.4 %fusion.45 = f32[2048,512]{1,0:T(8,128)S(1)} fusion(f32[16,512]{1,0:T(8,128)S(1)} %get-tuple-element.236, f32[16,16384]{1,0:T(8,128)} %get-tuple-element.235, s32[]{:T(128)S(6)} %select_n.100), kind=kOutput, calls=%fused_computation.23.clone.1 | convolution fusion | flops 201326592 | bytes 4358148 | tf_op jit(solution)/shard_map/while/body/eval_jaxpr/dot_general | solution.py:16
  154.3 4.8 %fusion.46 = f32[8,512]{1,0:T(8,128)S(1)} fusion(f32[2048,512]{1,0:T(8,128)S(1)} %fusion.45, f32[2048]{0:T(1024)S(1)} %multiply_reduce_fusion.3, f32[512]{0:T(512)S(1)} %get-tuple-element.234, f32[8,16384]{1,0:T(8,128)S(1)} %get-tuple-element.233, s32[]{:T(128)S(6)} %select_n.100, f32[8,512]{1,0:T(8,128)S(1)} %get-tuple-element.222, pred[]{:T(512)S(6)} %compare.3), kind=kOutput, calls=%fused_computation.21.clone.1 | convolution fusion | flops 112205824 | bytes 4302853 | tf_op jit(solution)/shard_map/while/body/eval_jaxpr/dot_general | solution.py:33
  159.1 0.9 multiply_reduce_fusion.3
  160.0 4.4 %fusion.45 = f32[2048,512]{1,0:T(8,128)S(1)} fusion(f32[16,512]{1,0:T(8,128)S(1)} %get-tuple-element.236, f32[16,16384]{1,0:T(8,128)} %get-tuple-element.235, s32[]{:T(128)S(6)} %select_n.100), kind=kOutput, calls=%fused_computation.23.clone.1 | convolution fusion | flops 201326592 | bytes 4358148 | tf_op jit(solution)/shard_map/while/body/eval_jaxpr/dot_general | solution.py:16
  164.4 4.8 %fusion.46 = f32[8,512]{1,0:T(8,128)S(1)} fusion(f32[2048,512]{1,0:T(8,128)S(1)} %fusion.45, f32[2048]{0:T(1024)S(1)} %multiply_reduce_fusion.3, f32[512]{0:T(512)S(1)} %get-tuple-element.234, f32[8,16384]{1,0:T(8,128)S(1)} %get-tuple-element.233, s32[]{:T(128)S(6)} %select_n.100, f32[8,512]{1,0:T(8,128)S(1)} %get-tuple-element.222, pred[]{:T(512)S(6)} %compare.3), kind=kOutput, calls=%fused_computation.21.clone.1 | convolution fusion | flops 112205824 | bytes 4302853 | tf_op jit(solution)/shard_map/while/body/eval_jaxpr/dot_general | solution.py:33
  169.2 0.9 multiply_reduce_fusion.3
  170.2 4.4 %fusion.45 = f32[2048,512]{1,0:T(8,128)S(1)} fusion(f32[16,512]{1,0:T(8,128)S(1)} %get-tuple-element.236, f32[16,16384]{1,0:T(8,128)} %get-tuple-element.235, s32[]{:T(128)S(6)} %select_n.100), kind=kOutput, calls=%fused_computation.23.clone.1 | convolution fusion | flops 201326592 | bytes 4358148 | tf_op jit(solution)/shard_map/while/body/eval_jaxpr/dot_general | solution.py:16
  174.6 4.8 %fusion.46 = f32[8,512]{1,0:T(8,128)S(1)} fusion(f32[2048,512]{1,0:T(8,128)S(1)} %fusion.45, f32[2048]{0:T(1024)S(1)} %multiply_reduce_fusion.3, f32[512]{0:T(512)S(1)} %get-tuple-element.234, f32[8,16384]{1,0:T(8,128)S(1)} %get-tuple-element.233, s32[]{:T(128)S(6)} %select_n.100, f32[8,512]{1,0:T(8,128)S(1)} %get-tuple-element.222, pred[]{:T(512)S(6)} %compare.3), kind=kOutput, calls=%fused_computation.21.clone.1 | convolution fusion | flops 112205824 | bytes 4302853 | tf_op jit(solution)/shard_map/while/body/eval_jaxpr/dot_general | solution.py:33
  179.4 0.9 multiply_reduce_fusion.3
  180.3 4.4 %fusion.45 = f32[2048,512]{1,0:T(8,128)S(1)} fusion(f32[16,512]{1,0:T(8,128)S(1)} %get-tuple-element.236, f32[16,16384]{1,0:T(8,128)} %get-tuple-element.235, s32[]{:T(128)S(6)} %select_n.100), kind=kOutput, calls=%fused_computation.23.clone.1 | convolution fusion | flops 201326592 | bytes 4358148 | tf_op jit(solution)/shard_map/while/body/eval_jaxpr/dot_general | solution.py:16
  184.7 4.8 %fusion.46 = f32[8,512]{1,0:T(8,128)S(1)} fusion(f32[2048,512]{1,0:T(8,128)S(1)} %fusion.45, f32[2048]{0:T(1024)S(1)} %multiply_reduce_fusion.3, f32[512]{0:T(512)S(1)} %get-tuple-element.234, f32[8,16384]{1,0:T(8,128)S(1)} %get-tuple-element.233, s32[]{:T(128)S(6)} %select_n.100, f32[8,512]{1,0:T(8,128)S(1)} %get-tuple-element.222, pred[]{:T(512)S(6)} %compare.3), kind=kOutput, calls=%fused_computation.21.clone.1 | convolution fusion | flops 112205824 | bytes 4302853 | tf_op jit(solution)/shard_map/while/body/eval_jaxpr/dot_general | solution.py:33
  189.5 0.9 multiply_reduce_fusion.3
  190.5 4.4 %fusion.45 = f32[2048,512]{1,0:T(8,128)S(1)} fusion(f32[16,512]{1,0:T(8,128)S(1)} %get-tuple-element.236, f32[16,16384]{1,0:T(8,128)} %get-tuple-element.235, s32[]{:T(128)S(6)} %select_n.100), kind=kOutput, calls=%fused_computation.23.clone.1 | convolution fusion | flops 201326592 | bytes 4358148 | tf_op jit(solution)/shard_map/while/body/eval_jaxpr/dot_general | solution.py:16
  194.9 4.8 %fusion.46 = f32[8,512]{1,0:T(8,128)S(1)} fusion(f32[2048,512]{1,0:T(8,128)S(1)} %fusion.45, f32[2048]{0:T(1024)S(1)} %multiply_reduce_fusion.3, f32[512]{0:T(512)S(1)} %get-tuple-element.234, f32[8,16384]{1,0:T(8,128)S(1)} %get-tuple-element.233, s32[]{:T(128)S(6)} %select_n.100, f32[8,512]{1,0:T(8,128)S(1)} %get-tuple-element.222, pred[]{:T(512)S(6)} %compare.3), kind=kOutput, calls=%fused_computation.21.clone.1 | convolution fusion | flops 112205824 | bytes 4302853 | tf_op jit(solution)/shard_map/while/body/eval_jaxpr/dot_general | solution.py:33
  199.7 0.9 multiply_reduce_fusion.3
  200.6 4.4 %fusion.45 = f32[2048,512]{1,0:T(8,128)S(1)} fusion(f32[16,512]{1,0:T(8,128)S(1)} %get-tuple-element.236, f32[16,16384]{1,0:T(8,128)} %get-tuple-element.235, s32[]{:T(128)S(6)} %select_n.100), kind=kOutput, calls=%fused_computation.23.clone.1 | convolution fusion | flops 201326592 | bytes 4358148 | tf_op jit(solution)/shard_map/while/body/eval_jaxpr/dot_general | solution.py:16
  205.0 4.8 %fusion.46 = f32[8,512]{1,0:T(8,128)S(1)} fusion(f32[2048,512]{1,0:T(8,128)S(1)} %fusion.45, f32[2048]{0:T(1024)S(1)} %multiply_reduce_fusion.3, f32[512]{0:T(512)S(1)} %get-tuple-element.234, f32[8,16384]{1,0:T(8,128)S(1)} %get-tuple-element.233, s32[]{:T(128)S(6)} %select_n.100, f32[8,512]{1,0:T(8,128)S(1)} %get-tuple-element.222, pred[]{:T(512)S(6)} %compare.3), kind=kOutput, calls=%fused_computation.21.clone.1 | convolution fusion | flops 112205824 | bytes 4302853 | tf_op jit(solution)/shard_map/while/body/eval_jaxpr/dot_general | solution.py:33
  209.8 0.0 copy-start.1
  209.8 0.6 copy-done.1
  (8 shorter events, 0.0 us)
Async XLA Ops:
  6.5 6.4 %copy-start = (s32[16,16]{1,0:T(8,128)S(1)}, s32[16,16]{1,0:T(8,128)}, u32[]{:S(2)}) copy-start(s32[16,16]{1,0:T(8,128)} %param.10) | copy-start | bytes 3076
  6.5 122.1 %all-gather.2.cloned.1.call-start = ((), (), s32[]{:S(2)}) async-start(), calls=%async_computation | async-start | bytes 1081344 | tf_op jit(solution)/shard_map/all_gather | solution.py:56
  7.4 6.1 %collective-permute-start.4 = (f32[16,512]{1,0:T(8,128)S(1)}, f32[16,512]{1,0:T(8,128)S(1)}, u32[]{:S(2)}, u32[]{:S(2)}) collective-permute-start(f32[16,512]{1,0:T(8,128)S(1)} %get-tuple-element.216), channel_id=1, source_target_pairs={{0,32},{32,0},{64,96},{96,64},{128,160},{160,128},{192,224},{224,1... | collective-permute-start | bytes 98312 | tf_op jit(solution)/shard_map/ppermute | solution.py:12
  13.5 7.1 %collective-permute-start.5 = (f32[16,512]{1,0:T(8,128)S(1)}, f32[16,512]{1,0:T(8,128)S(1)}, u32[]{:S(2)}, u32[]{:S(2)}) collective-permute-start(f32[16,512]{1,0:T(8,128)S(1)} %broadcast_select_fusion), channel_id=1, source_target_pairs={{0,64},{32,96},{64,0},{96,32},{128,192},{160,224},{192,128},{224,1... | collective-permute-start | bytes 98312 | tf_op jit(solution)/shard_map/ppermute | solution.py:12
  20.6 4.6 %collective-permute-start.6 = (f32[16,512]{1,0:T(8,128)S(1)}, f32[16,512]{1,0:T(8,128)S(1)}, u32[]{:S(2)}, u32[]{:S(2)}) collective-permute-start(f32[16,512]{1,0:T(8,128)S(1)} %broadcast_select_fusion.1), channel_id=1, source_target_pairs={{0,128},{32,160},{64,192},{96,224},{128,0},{160,32},{192,64},{224,... | collective-permute-start | bytes 98312 | tf_op jit(solution)/shard_map/ppermute | solution.py:12
  25.3 6.2 %collective-permute-start.7 = (f32[16,512]{1,0:T(8,128)S(1)}, f32[16,512]{1,0:T(8,128)S(1)}, u32[]{:S(2)}, u32[]{:S(2)}) collective-permute-start(f32[16,512]{1,0:T(8,128)S(1)} %broadcast_select_fusion.2), channel_id=1, source_target_pairs={{0,256},{32,288},{64,320},{96,352},{128,384},{160,416},{192,448},{... | collective-permute-start | bytes 98312 | tf_op jit(solution)/shard_map/ppermute | solution.py:12
  32.1 4.7 %collective-permute-start = (f32[8,512]{1,0:T(8,128)}, f32[8,512]{1,0:T(8,128)S(1)}, u32[]{:S(2)}, u32[]{:S(2)}) collective-permute-start(f32[8,512]{1,0:T(8,128)} %param.9), channel_id=1, source_target_pairs={{0,32},{32,0},{64,96},{96,64},{128,160},{160,128},{192,224},{224,1... | collective-permute-start | bytes 49160 | tf_op jit(solution)/shard_map/ppermute | solution.py:12
  37.5 5.5 %collective-permute-start.1 = (f32[8,512]{1,0:T(8,128)S(1)}, f32[8,512]{1,0:T(8,128)S(1)}, u32[]{:S(2)}, u32[]{:S(2)}) collective-permute-start(f32[8,512]{1,0:T(8,128)S(1)} %broadcast_select_fusion.4), channel_id=1, source_target_pairs={{0,64},{32,96},{64,0},{96,32},{128,192},{160,224},{192,128},{224,1... | collective-permute-start | bytes 49160 | tf_op jit(solution)/shard_map/ppermute | solution.py:12
  43.0 4.5 %collective-permute-start.2 = (f32[8,512]{1,0:T(8,128)S(1)}, f32[8,512]{1,0:T(8,128)S(1)}, u32[]{:S(2)}, u32[]{:S(2)}) collective-permute-start(f32[8,512]{1,0:T(8,128)S(1)} %broadcast_select_fusion.5), channel_id=1, source_target_pairs={{0,128},{32,160},{64,192},{96,224},{128,0},{160,32},{192,64},{224,... | collective-permute-start | bytes 49160 | tf_op jit(solution)/shard_map/ppermute | solution.py:12
  47.5 6.0 %collective-permute-start.3 = (f32[8,512]{1,0:T(8,128)S(1)}, f32[8,512]{1,0:T(8,128)S(1)}, u32[]{:S(2)}, u32[]{:S(2)}) collective-permute-start(f32[8,512]{1,0:T(8,128)S(1)} %broadcast_select_fusion.6), channel_id=1, source_target_pairs={{0,256},{32,288},{64,320},{96,352},{128,384},{160,416},{192,448},{... | collective-permute-start | bytes 49160 | tf_op jit(solution)/shard_map/ppermute | solution.py:12
  209.8 0.6 copy-start.1
Sparse Core Ops, SparseCore 0:
  32.2 96.4 all-gather.1
where the time goes:
time: 218 us; the launch traced here: 217 us
  matrix products  73.6 us (34%)
  blocking collectives  67.7 us (31%)
  starting transfers between devices  33.7 us (15%)
  waiting for transfers between devices  17.5 us (8%)
  between operations  14.3 us (7%)
  other arithmetic  9.72 us (4%)
    all_gather x1, blocking collectives, shards(): vecs = lax.all_gather(far_prb, 'mem', axis=1, tiled=True)  67.7 us
    dot_general x8, matrix products, apply_probes(): lax.dot_general(vectors, kern, (((1,), (1,)), ((), ())), precision=lax.Pr...  38.5 us
    dot_general x8, matrix products, matern(): lax.dot_general(left, right, (((0,), (0,)), ((), ())), precision=lax.Prec...  35.1 us
    ppermute x8, starting transfers between devices, swapped(): lax.ppermute(x, axis, [(i, i ^ 1 << bit) for i in range(lax.axis_size(axi...  33.7 us
    ppermute x8, waiting for transfers between devices, swapped(): lax.ppermute(x, axis, [(i, i ^ 1 << bit) for i in range(lax.axis_size(axi...  10.1 us
    reduce_sum x8, other arithmetic, matern(): jnp.sum(right * right, axis=0)[None, :]  7.49 us
    all_gather x1, waiting for transfers between devices, shards(): cols = lax.all_gather(far_pts, 'mem', axis=1, tiled=True)  7.44 us
  transfers between devices with their start and end apart: 9, of which 9 were waited for; matrix products, arithmetic and copies ran while one was open for 0% of the time, Pallas kernels for 0%

commit v1 on v0

v1 whole, which is shorter than its diff:
```python
import functools
import math

import jax
import jax.numpy as jnp
from jax import lax
from jax.experimental import pallas as pl
from jax.experimental.pallas import tpu as pltpu
from jax.sharding import PartitionSpec as P

F32, BF16 = jnp.float32, jnp.bfloat16
MESH = pl.DeviceIdType.MESH
LOG2E = math.log2(math.e)
UNIT = math.sqrt(LOG2E / 3.0)
SCALE = math.sqrt(5.0) * UNIT
SLOPE = -LOG2E / UNIT
SHIFT = 3.0 * UNIT * UNIT

FEAT, PROBES, PTS = 16, 8, 512
ROWS = FEAT + PROBES
DEPTH = 128
RING, CORES, HALVES = 8, 2, 2
BLOCKS = RING * CORES * HALVES


def swap_kernel(shift, ls_ref, pts_ref, prb_ref, own_ref, far_ref, send_sem, recv_sem):
    grp, mem = lax.axis_index("grp"), lax.axis_index("mem")
    partner = grp
    for bit in range(4):
        if shift >> bit & 1:
            partner = partner + (1 - 2 * ((grp // (1 << bit)) % 2)) * (1 << bit)
    barrier = pltpu.get_barrier_semaphore()
    pl.semaphore_signal(barrier, inc=1, device_id=(partner, mem), device_id_type=MESH)
    row = lax.broadcasted_iota(jnp.int32, (FEAT, PTS), 0)
    scales = jnp.full((FEAT, PTS), ls_ref[0], F32)
    for feature in range(1, FEAT):
        scales = jnp.where(row == feature, ls_ref[feature], scales)
    own_ref[0:FEAT, :] = pts_ref[...] / scales * SCALE
    own_ref[FEAT:ROWS, :] = prb_ref[...]
    pl.semaphore_wait(barrier, 1)
    copy = pltpu.make_async_remote_copy(
        src_ref=own_ref,
        dst_ref=far_ref,
        send_sem=send_sem,
        recv_sem=recv_sem,
        device_id=(partner, mem),
        device_id_type=MESH,
    )
    copy.start()
    copy.wait()


def swap(shift, ls, points, probes):
    vmem = pl.BlockSpec(memory_space=pltpu.VMEM)
    return pl.pallas_call(
        functools.partial(swap_kernel, shift),
        out_shape=[jax.ShapeDtypeStruct((ROWS, PTS), F32)] * 2,
        in_specs=[pl.BlockSpec(memory_space=pltpu.SMEM), vmem, vmem],
        out_specs=[vmem, vmem],
        scratch_shapes=[pltpu.SemaphoreType.DMA, pltpu.SemaphoreType.DMA],
        compiler_params=pltpu.CompilerParams(collective_id=shift, has_side_effects=True),
        name="swap",
    )(ls, points, probes)


def pieces(x):
    first = x.astype(BF16)
    rest = x - first.astype(F32)
    second = rest.astype(BF16)
    third = (rest - second.astype(F32)).astype(BF16)
    return first, second, third


def lifted(x, left):
    norm = jnp.sum(x * x, axis=0, keepdims=True)
    if left:
        x = x * -2.0
    a, b, c = pieces(x)
    row = lax.broadcasted_iota(jnp.int32, (FEAT, PTS), 0)
    first = 0 if left else 3
    ones = jnp.logical_and(row >= 3 - first, row < 6 - first)
    tail = jnp.where(ones, 1.0, 0.0)
    for index, part in enumerate(pieces(norm)):
        tail = jnp.where(row == first + index, jnp.broadcast_to(part.astype(F32), tail.shape), tail)
    tail = tail.astype(BF16)
    rows = [a, a, b, a, b, c] if left else [a, b, a, c, b, a]
    return jnp.concatenate(rows + [tail, jnp.zeros_like(tail)], 0)


def dot(a, b):
    return lax.dot_general(a, b, (((1,), (0,)), ((), ())), preferred_element_type=F32)


def matern(dist):
    t = jnp.maximum(dist, 1e-30)
    y = t * lax.rsqrt(t) * SLOPE
    return (t - y + SHIFT) * jnp.exp2(y)


UNITS = [
    (0, 0), (-1, 0), (1, 0), (0, 1), (-2, 0), (2, 0), (-1, 1), (1, 1),
    (-3, 0), (3, 0), (-2, 1), (2, 1), (4, 0), (-3, 1), (3, 1), (4, 1),
]
UP_LIMIT = (4, 3)
DOWN_LIMIT = (3, 4)


def block_kernel(
    own_ref, far_ref, out_ref,
    land, left, t0, t1, d0, d1, h0, h1, l0, l1, p0, p1, acc,
    recv_sem, y_sem, sib_sem, z_sem,
):
    grp, mem = lax.axis_index("grp"), lax.axis_index("mem")
    half, ring, core = mem // (RING * CORES), (mem // CORES) % RING, mem % CORES

    def member(h, r, c):
        return (grp, (h * RING + r) * CORES + c)

    up, down = (ring + 1) % RING, (ring + RING - 1) % RING
    to_up, to_down = member(half, up, core), member(half, down, core)
    to_half, to_core = member(1 - half, ring, core), member(half, ring, 1 - core)

    def slot(unit, other_core):
        offset, other_half = UNITS[unit]
        c = 1 - core if other_core else core
        h = 1 - half if other_half else half
        return ((ring + offset + RING) % RING * CORES + c) * HALVES + h

    def copy(where, send_sem, device):
        return pltpu.make_async_remote_copy(
            src_ref=land.at[where],
            dst_ref=land.at[where],
            send_sem=send_sem,
            recv_sem=recv_sem.at[where],
            device_id=device,
            device_id_type=MESH,
        )

    def sends(unit):
        offset, other = UNITS[unit]
        where = slot(unit, False)
        out = [copy(where, sib_sem.at[unit], to_core)]
        if unit == 0:
            out.append(copy(where, z_sem, to_half))
        if -UP_LIMIT[other] < offset <= 0:
            out.append(copy(where, y_sem.at[unit, 0], to_up))
        if 0 <= offset < DOWN_LIMIT[other] and not (offset == 4):
            out.append(copy(where, y_sem.at[unit, 1], to_down))
        return out

    def arrived(where):
        copy(where, z_sem, to_half).wait_recv()

    barrier = pltpu.get_barrier_semaphore()
    for device in (to_up, to_down, to_half, to_core):
        pl.semaphore_signal(barrier, inc=1, device_id=device, device_id_type=MESH)
    land[slot(0, False)] = far_ref[...]
    left[...] = lifted(own_ref[0:FEAT, :], True)
    acc[...] = jnp.zeros_like(acc)
    h1[...] = jnp.zeros_like(h1)
    l1[...] = jnp.zeros_like(l1)
    p1[...] = jnp.zeros_like(p1)
    T, D, H, L, W = (t0, t1), (d0, d1), (h0, h1), (l0, l1), (p0, p1)

    def lift(where, k):
        T[k][...] = lifted(land[where, 0:FEAT, :], False).T

    def distances(k):
        D[k][...] = dot(T[k][...], left[...])

    def step(where, ahead, k):
        o = 1 - k
        for r in range(0, PTS, 256):
            for c in range(0, PTS, 256):
                rows, cols = slice(r, r + 256), slice(c, c + 256)
                value = matern(D[k][rows, cols])
                high = value.astype(BF16)
                H[k][rows, cols] = high
                L[k][rows, cols] = (value - high.astype(F32)).astype(BF16)
                D[o][rows, cols] = dot(T[o][rows, :], left[:, cols])
                weights = W[o][:, rows]
                acc[:, cols] += dot(weights, H[o][rows, cols]) + dot(weights, L[o][rows, cols])
        probes = land[where, FEAT:ROWS, :]
        high = probes.astype(BF16)
        W[k][...] = jnp.concatenate([high, (probes - high.astype(F32)).astype(BF16)], 0)
        lift(ahead, k)

    pl.semaphore_wait(barrier, 4)
    for item in sends(0):
        item.start()
    lift(slot(0, False), 0)
    distances(0)
    arrived(slot(0, True))
    lift(slot(0, True), 1)

    def picked(index, values):
        result = values[0]
        for at in range(1, len(values)):
            result = jnp.where(index == at, values[at], result)
        return result

    n_units = len(UNITS)
    slots = [slot(unit, other) for unit in range(n_units) for other in (False, True)]
    slots += [slots[-2], slots[-1]]

    def body(n, carry):
        for m in range(n_units // 2):
            @pl.when(n == m)
            def _():
                for unit in (2 * m + 1, 2 * m + 2):
                    if unit < n_units:
                        arrived(slot(unit, False))
                        for item in sends(unit):
                            item.start()
                for unit in (2 * m + 1, 2 * m + 2):
                    if unit < n_units:
                        arrived(slot(unit, True))
        here = [picked(n, slots[at::4][:n_units // 2]) for at in range(4)]
        ahead = here[2:] + [picked(n, slots[at + 4::4][:n_units // 2]) for at in range(2)]
        for q in range(4):
            step(here[q], ahead[q], q % 2)
        return carry

    lax.fori_loop(0, n_units // 2, body, 0)
    acc[...] += dot(p1[...], h1[...]) + dot(p1[...], l1[...])
    out_ref[...] = (acc[0:PROBES, :] + acc[PROBES : 2 * PROBES, :]) * (1.0 / SHIFT)
    for unit in range(n_units):
        for item in sends(unit):
            item.wait_send()


def blocks(own, far):
    vmem = pl.BlockSpec(memory_space=pltpu.VMEM)
    return pl.pallas_call(
        block_kernel,
        out_shape=jax.ShapeDtypeStruct((PROBES, PTS), F32),
        in_specs=[vmem, vmem],
        out_specs=vmem,
        scratch_shapes=[
            pltpu.VMEM((BLOCKS, ROWS, PTS), F32),
            pltpu.VMEM((DEPTH, PTS), BF16),
            pltpu.VMEM((PTS, DEPTH), BF16),
            pltpu.VMEM((PTS, DEPTH), BF16),
            pltpu.VMEM((PTS, PTS), F32),
            pltpu.VMEM((PTS, PTS), F32),
            pltpu.VMEM((PTS, PTS), BF16),
            pltpu.VMEM((PTS, PTS), BF16),
            pltpu.VMEM((PTS, PTS), BF16),
            pltpu.VMEM((PTS, PTS), BF16),
            pltpu.VMEM((2 * PROBES, PTS), BF16),
            pltpu.VMEM((2 * PROBES, PTS), BF16),
            pltpu.VMEM((2 * PROBES, PTS), F32),
            pltpu.SemaphoreType.DMA((BLOCKS,)),
            pltpu.SemaphoreType.DMA((len(UNITS), 2)),
            pltpu.SemaphoreType.DMA((len(UNITS),)),
            pltpu.SemaphoreType.DMA,
        ],
        compiler_params=pltpu.CompilerParams(
            collective_id=0, has_side_effects=True, vmem_limit_bytes=32 << 20
        ),
        name="blocks",
    )(own, far)


def shards(points, lengthscales, probes, plan, round_index):
    shift = plan[round_index[0], 0]
    own, far = lax.switch(
        shift - 1,
        [functools.partial(swap, which) for which in range(1, 16)],
        lengthscales, points, probes,
    )
    return blocks(own, far)


def solution(mesh):
    in_specs = (P(None, ("grp", "mem")), P(), P(None, ("grp", "mem")), P(), P())
    out_specs = P(None, ("grp", "mem"))
    return jax.shard_map(shards, mesh=mesh, in_specs=in_specs, out_specs=out_specs, check_vma=False)
```

time: 218 us -> 53.1 us (0.24)
  matrix products: 73.6 us -> 0 us
  blocking collectives: 67.7 us -> 0 us
  Pallas kernels: 0 us -> 48.9 us
  starting transfers between devices: 33.7 us -> 0 us
  waiting for transfers between devices: 17.5 us -> 0 us
  between operations: 14.3 us -> 1.35 us
  other arithmetic: 9.72 us -> 1.21 us
    dot_general x16 -> x0, matrix products: 73.6 us -> none  [the longest x8 38.5 us: apply_probes(): lax.dot_general(vectors, kern, (((1,), (1,)), ((), ())), precision=lax.Pr...]
    all_gather x1 -> x0, blocking collectives: 67.7 us -> none  [shards(): vecs = lax.all_gather(far_prb, 'mem', axis=1, tiled=True)]
    pallas_call x0 -> x2, Pallas kernels: none -> 48.9 us  [the longest x1 43 us: blocks(): pl.pallas_call(block_kernel, out_shape=jax.ShapeDtypeStruct((PROBES, PTS)...]
    ppermute x8 -> x0, starting transfers between devices: 33.7 us -> none  [swapped(): lax.ppermute(x, axis, [(i, i ^ 1 << bit) for i in range(lax.axis_size(axi...]
    ppermute x8 -> x0, waiting for transfers between devices: 10.1 us -> none  [swapped(): lax.ppermute(x, axis, [(i, i ^ 1 << bit) for i in range(lax.axis_size(axi...]
    reduce_sum x9 -> x0, other arithmetic: 8.35 us -> none  [the longest x8 7.49 us: matern(): jnp.sum(right * right, axis=0)[None, :]]
    all_gather x1 -> x0, waiting for transfers between devices: 7.44 us -> none  [shards(): cols = lax.all_gather(far_pts, 'mem', axis=1, tiled=True)]
  transfers between devices with their start and end apart: 9 -> 0, of which waited for: 9 -> 0; matrix products, arithmetic and copies ran while one was open for 0% -> 0% of each run, Pallas kernels for 0% -> 0%
where the time goes in v1:
time: 53.1 us; the launch traced here: 52.8 us
  Pallas kernels  48.9 us (92%)
  between operations  1.35 us (3%)
  local copies, waits for them, and re-layouts  1.25 us (2%)
  other arithmetic  1.21 us (2%)
    pallas_call x1, Pallas kernels, blocks(): pl.pallas_call(block_kernel, out_shape=jax.ShapeDtypeStruct((PROBES, PTS)...  43 us
    pallas_call x1, Pallas kernels, swap(): pl.pallas_call(functools.partial(swap_kernel, shift), out_shape=[jax.Shap...  5.91 us
    unnamed x5, local copies, waits for them, and re-layouts  1.25 us
    sub x1, other arithmetic, shards(): shift - 1  1.21 us

profile of v1, /device:TPU:1, one launch (start us, length us, event | category | flops | bytes accessed | tf_op | source)
XLA Modules:
  0.0 52.8 jit_solution(6488154964515496941)
XLA Ops:
  0.0 0.0 copy-start
  0.7 1.2 %fusion = s32[1,1]{1,0:T(1,128)} fusion(s32[16,16]{1,0:T(8,128)} %param.23, s32[]{:T(128)S(6)} %select_n.3), kind=kLoop, calls=%fused_computation.1 | loop fusion | flops 1 | bytes 12 | tf_op jit(solution)/shard_map/sub | solution.py:268
  2.5 0.0 copy-start.1
  2.5 0.0 copy-done
  2.5 0.6 %copy-done.1 = f32[16]{0:T(128)S(1)} copy-done((f32[16]{0:T(128)S(1)}, f32[16]{0:T(128)}, u32[]{:S(2)}) %copy-start.1) | copy-done | bytes 88
  3.2 5.9 %conditional.1 = ((f32[24,512]{1,0:T(8,128)S(1)}, f32[24,512]{1,0:T(8,128)S(1)})) conditional(s32[]{:T(128)} %bitcast.1, (f32[16]{0:T(128)S(1)}, f32[16,512]{1,0:T(8,128)}, f32[8,512]{1,0:T(8,128)S(1)}) %tuple.96, (f32[16]{0:T(128)S(1)}, f32[16,512]{1,0:T(8,128)}, f32[8,512]{1,0:T(8,128)S(1)}) %tuple.97, ...), branch_computations={%region_0.0_spmd, %region_1.0_spmd, %region_2.0_spmd, %region_3.0_... | conditional | bytes 8 | solution.py:267
  3.2 5.9 %swap.15 = (f32[24,512]{1,0:T(8,128)S(1)}, f32[24,512]{1,0:T(8,128)S(1)}) custom-call(f32[16]{0:T(128)S(1)} %get-tuple-element.95.ls_ref, f32[16,512]{1,0:T(8,128)} %get-tuple-element.96.pts_ref, f32[8,512]{1,0:T(8,128)S(1)} %get-tuple-element.97.prb_ref), custom_call_target="tpu_custom_call" | custom-call | tf_op jit(solution)/shard_map/cond/branch_0_fun/swap/pallas_call | solution.py:55
  9.1 43.0 %blocks.1 = f32[8,512]{1,0:T(8,128)S(1)} custom-call(f32[24,512]{1,0:T(8,128)S(1)} %get-tuple-element.142.own_ref, f32[24,512]{1,0:T(8,128)S(1)} %get-tuple-element.143.far_ref), custom_call_target="tpu_custom_call" | custom-call | tf_op jit(solution)/shard_map/blocks/pallas_call | solution.py:234
  52.2 0.6 %copy.38 = f32[8,512]{1,0:T(8,128)} copy(f32[8,512]{1,0:T(8,128)S(1)} %blocks.1) | data formatting | bytes 32768
Async XLA Ops:
  0.0 2.5 %copy-start = (f32[8,512]{1,0:T(8,128)S(1)}, f32[8,512]{1,0:T(8,128)}, u32[]{:S(2)}) copy-start(f32[8,512]{1,0:T(8,128)} %param.22) | copy-start | bytes 49156
  2.5 0.7 %copy-start.1 = (f32[16]{0:T(128)S(1)}, f32[16]{0:T(128)}, u32[]{:S(2)}) copy-start(f32[16]{0:T(128)} %param.21) | copy-start | bytes 196
